TPU v7x, 32 devices: a whole 2x2x4 slice. The times are simulated.
32 devices in a mesh: row: 4 (over y, x), col: 8 (over z, core).
Axes of the slice: x: 2, y: 2, z: 4, core: 2. Of those that a mesh axis runs over, the one named last changes fastest.
Arguments:
- tokens: bfloat16 [128, 256, 1024], P(('row', 'col')), may hold values from -7 to 7
- phi: bfloat16 [1024, 32], replicated, may hold values from -5 to 5
- w_in: bfloat16 [32, 1024, 2048], P(('row', 'col')), may hold values from -0.1875 to 0.1875
- w_out: bfloat16 [32, 2048, 1024], P(('row', 'col')), may hold values from -0.125 to 0.125
- cotangent: bfloat16 [128, 256, 1024], P(('row', 'col')), may hold values from -6 to 6
Outputs:
- mixed: bfloat16 [128, 256, 1024], P(('row', 'col'))
- grad_tokens: bfloat16 [128, 256, 1024], P(('row', 'col'))
- grad_phi: float32 [1024, 32], P(None, ('row', 'col'))
- grad_w_in: bfloat16 [32, 1024, 2048], P(('row', 'col'))
- grad_w_out: bfloat16 [32, 2048, 1024], P(('row', 'col'))
All inputs are finite; a program needn't handle non-finite values.
Results may differ from a plain program's by a relative error of at most 0.015.
Values may be sent and summed in bfloat16 or wider, within the bound.
A program may use at most 128 MiB of HBM per device.

v0:
```python
import math
import jax
import jax.numpy as jnp
from jax import lax
from jax.sharding import PartitionSpec as P


def gelu_parts(pre_act):
    const = math.sqrt(2.0 / math.pi)
    inner = const * (pre_act + 0.044715 * pre_act**3)
    tanh_val = jnp.tanh(inner)
    value = 0.5 * pre_act * (1.0 + tanh_val)
    slope = 0.5 * (1.0 + tanh_val) + 0.5 * pre_act * (1.0 - tanh_val * tanh_val) * const * (
        1.0 + 3.0 * 0.044715 * pre_act * pre_act
    )
    return (value, slope)


def send_slots(slots):
    return lax.all_to_all(slots, ("row", "col"), split_axis=1, concat_axis=1, tiled=True)


def return_results(slots):
    return lax.all_to_all(slots, ("row", "col"), split_axis=1, concat_axis=1, tiled=True)


def send_out_grads(slots):
    return lax.all_to_all(slots, ("row", "col"), split_axis=1, concat_axis=1, tiled=True)


def return_in_grads(slots):
    return lax.all_to_all(slots, ("row", "col"), split_axis=1, concat_axis=1, tiled=True)


def on_device(tokens, phi, w_in, w_out, cotangent):
    f32 = jnp.float32
    images, patches, feature_dim = tokens.shape
    logits = jnp.einsum("imd,ds->ims", tokens, phi, preferred_element_type=f32)
    dispatch = jax.nn.softmax(logits, axis=1)
    combine = jax.nn.softmax(logits, axis=2)
    dispatch_b = dispatch.astype(jnp.bfloat16)
    combine_b = combine.astype(jnp.bfloat16)
    slot_in = jnp.einsum("ims,imd->isd", dispatch_b, tokens, preferred_element_type=f32).astype(
        jnp.bfloat16
    )
    expert_in = send_slots(slot_in)
    expert_rows = expert_in.reshape(-1, feature_dim)
    weight_a = w_in[0]
    weight_b = w_out[0]
    pre_act = jnp.dot(expert_rows, weight_a, preferred_element_type=f32)
    value, slope = gelu_parts(pre_act)
    hidden = value.astype(jnp.bfloat16)
    expert_out = jnp.dot(hidden, weight_b, preferred_element_type=f32).astype(jnp.bfloat16)
    slot_out = return_results(expert_out.reshape(expert_in.shape))
    mixed = jnp.einsum("ims,isd->imd", combine_b, slot_out, preferred_element_type=f32).astype(
        jnp.bfloat16
    )
    d_slot_out = jnp.einsum(
        "ims,imd->isd", combine_b, cotangent, preferred_element_type=f32
    ).astype(jnp.bfloat16)
    grad_rows = send_out_grads(d_slot_out).reshape(-1, feature_dim)
    d_combine = jnp.einsum("imd,isd->ims", cotangent, slot_out, preferred_element_type=f32)
    d_logits_c = combine * (d_combine - jnp.sum(combine * d_combine, axis=2, keepdims=True))
    grad_b = jnp.einsum("rh,rd->hd", hidden, grad_rows, preferred_element_type=f32).astype(
        jnp.bfloat16
    )
    d_hidden = jnp.einsum("rd,hd->rh", grad_rows, weight_b, preferred_element_type=f32)
    d_pre = (d_hidden * slope).astype(jnp.bfloat16)
    grad_a = jnp.einsum("rd,rh->dh", expert_rows, d_pre, preferred_element_type=f32).astype(
        jnp.bfloat16
    )
    d_rows = jnp.einsum("rh,dh->rd", d_pre, weight_a, preferred_element_type=f32).astype(
        jnp.bfloat16
    )
    d_slot_in = return_in_grads(d_rows.reshape(expert_in.shape))
    d_dispatch = jnp.einsum("imd,isd->ims", tokens, d_slot_in, preferred_element_type=f32)
    d_logits = (
        d_logits_c + dispatch * (d_dispatch - jnp.sum(dispatch * d_dispatch, axis=1, keepdims=True))
    ).astype(jnp.bfloat16)
    grad_tokens = (
        jnp.einsum("ims,isd->imd", dispatch_b, d_slot_in, preferred_element_type=f32)
        + jnp.einsum("ims,ds->imd", d_logits, phi, preferred_element_type=f32)
    ).astype(jnp.bfloat16)
    phi_terms = jnp.einsum("imd,ims->ds", tokens, d_logits, preferred_element_type=f32)
    grad_phi = lax.psum_scatter(phi_terms, ("row", "col"), scatter_dimension=1, tiled=True)
    return (mixed, grad_tokens, grad_phi, grad_a[None], grad_b[None])


def solution(mesh):
    placed = (
        P(("row", "col"), None, None),
        P(),
        P(("row", "col"), None, None),
        P(("row", "col"), None, None),
        P(("row", "col"), None, None),
    )
    return jax.shard_map(
        on_device,
        mesh=mesh,
        in_specs=placed,
        out_specs=(
            P(("row", "col"), None, None),
            P(("row", "col"), None, None),
            P(None, ("row", "col")),
            P(("row", "col"), None, None),
            P(("row", "col"), None, None),
        ),
        check_vma=False,
    )
```

profile of v0, /device:TPU:0, one launch (start us, length us, event | category | flops | bytes accessed | tf_op | source)
XLA Modules:
  0.0 219.8 jit_solution(336582949832847394)
XLA Ops:
  7.2 0.0 copy-start
  7.2 1.6 copy-done
  8.8 1.6 fusion.52
  10.3 0.8 fusion.60
  11.1 0.5 convolution_convert_fusion.2
  11.6 0.9 copy.18
  12.5 7.3 %all-to-all-start = ((bf16[4,32,1024]{2,0,1:T(4,128)(2,1)}), bf16[4,32,1024]{2,0,1:T(4,128)(2,1)S(1)}, u32[]{:S(2)}, u32[]{:S(2)}) async-start(bf16[4,32,1024]{2,0,1:T(4,128)(2,1)} %copy.18), calls=%async_computation | async-start | bytes 524288 | tf_op jit(solution)/shard_map/all_to_all | solution.py:20
  19.8 0.7 fusion.61
  20.5 2.0 convolution_convert_fusion.1
  22.6 0.9 copy.22
  23.5 6.7 %all-to-all-done = bf16[4,32,1024]{2,0,1:T(4,128)(2,1)S(1)} async-done(((bf16[4,32,1024]{2,0,1:T(4,128)(2,1)}), bf16[4,32,1024]{2,0,1:T(4,128)(2,1)S(1)}, u32[]{:S(2)}, u32[]{:S(2)}) %all-to-all-start) | async-done | bytes 262176 | tf_op jit(solution)/shard_map/all_to_all | solution.py:20
  30.2 3.3 %all-to-all-start.2 = ((bf16[4,32,1024]{2,0,1:T(4,128)(2,1)}), bf16[4,32,1024]{2,0,1:T(4,128)(2,1)}, u32[]{:S(2)}, u32[]{:S(2)}) async-start(bf16[4,32,1024]{2,0,1:T(4,128)(2,1)} %copy.22), calls=%async_computation.2 | async-start | bytes 524288 | tf_op jit(solution)/shard_map/all_to_all | solution.py:28
  33.5 0.0 copy-start.7
  33.5 0.1 copy.19
  33.6 3.1 %fusion.10 = f32[128,2048]{1,0:T(8,128)S(1)} fusion(bf16[128,1024]{1,0:T(8,128)(2,1)S(1)} %bitcast.57, bf16[1,1024,2048]{2,1,0:T(8,128)(2,1)} %param.7), kind=kOutput, calls=%fused_computation.10 | convolution fusion | flops 536870912 | bytes 5505024 | tf_op jit(solution)/shard_map/dot_general | solution.py:50
  36.7 0.3 copy-done.7
  37.0 1.6 fusion.21
  38.6 5.3 %all-to-all-done.2 = bf16[4,32,1024]{2,0,1:T(4,128)(2,1)} async-done(((bf16[4,32,1024]{2,0,1:T(4,128)(2,1)}), bf16[4,32,1024]{2,0,1:T(4,128)(2,1)}, u32[]{:S(2)}, u32[]{:S(2)}) %all-to-all-start.2) | async-done | bytes 262176 | tf_op jit(solution)/shard_map/all_to_all | solution.py:28
  43.9 1.0 copy.23
  44.9 0.0 copy-start.2
  44.9 0.0 copy-start.6
  44.9 4.9 %fusion.15 = bf16[128,2048]{1,0:T(8,128)(2,1)} fusion(bf16[128,1024]{1,0:T(8,128)(2,1)S(1)} %bitcast.59, bf16[1,2048,1024]{2,1,0:T(8,128)(2,1)} %param.8, f32[128,2048]{1,0:T(8,128)S(1)} %fusion.10), kind=kOutput, calls=%fused_computation.16 | convolution fusion | flops 541851648 | bytes 6029312 | tf_op jit(solution)/shard_map/rd,hd->rh/dot_general | solution.py:67
  49.8 0.0 copy-done.2
  49.8 0.0 copy-done.6
  49.8 0.9 copy.20
  50.8 3.3 %all-to-all-start.1 = ((bf16[4,32,1024]{2,0,1:T(4,128)(2,1)}), bf16[4,32,1024]{2,0,1:T(4,128)(2,1)}, u32[]{:S(2)}, u32[]{:S(2)}) async-start(bf16[4,32,1024]{2,0,1:T(4,128)(2,1)} %copy.20), calls=%async_computation.1 | async-start | bytes 524288 | tf_op jit(solution)/shard_map/all_to_all | solution.py:24
  54.1 0.0 copy-start.1
  54.1 0.0 copy-start.3
  54.1 3.9 %fusion.18 = bf16[128,1024]{1,0:T(8,128)(2,1)S(1)} fusion(bf16[128,2048]{1,0:T(8,128)(2,1)} %fusion.15, bf16[1,1024,2048]{2,1,0:T(8,128)(2,1)} %param.7), kind=kOutput, calls=%fused_computation.22 | convolution fusion | flops 537001984 | bytes 4980736 | tf_op jit(solution)/shard_map/rh,dh->rd/dot_general | solution.py:72
  58.0 0.9 copy.24
  58.9 3.3 %convert_bitcast_fusion.1 = bf16[1,1024,2048]{2,1,0:T(8,128)(2,1)} fusion(bf16[128,1024]{1,0:T(8,128)(2,1)S(1)} %bitcast.58, bf16[128,2048]{1,0:T(8,128)(2,1)S(1)} %copy-done.1), kind=kOutput, calls=%fused_computation.13 | convolution fusion | flops 538968064 | bytes 4980736 | tf_op jit(solution)/shard_map/rd,rh->dh/dot_general | solution.py:69
  62.2 3.3 %convert_bitcast_fusion = bf16[1,2048,1024]{2,1,0:T(8,128)(2,1)} fusion(bf16[128,1024]{1,0:T(8,128)(2,1)S(1)} %bitcast.60, f32[128,2048]{1,0:T(8,128)S(1)} %fusion.10), kind=kOutput, calls=%fused_computation.12 | convolution fusion | flops 541327360 | bytes 5505024 | tf_op jit(solution)/shard_map/rh,rd->hd/dot_general | solution.py:64
  65.6 0.0 all-to-all-done.1
  65.6 5.8 %all-to-all-start.3 = ((bf16[4,32,1024]{2,0,1:T(4,128)(2,1)}), bf16[4,32,1024]{2,0,1:T(4,128)(2,1)S(1)}, u32[]{:S(2)}, u32[]{:S(2)}) async-start(bf16[4,32,1024]{2,0,1:T(4,128)(2,1)} %copy.24), calls=%async_computation.3 | async-start | bytes 524288 | tf_op jit(solution)/shard_map/all_to_all | solution.py:32
  71.3 0.2 all-reduce.3.cloned.1.call-start
  71.6 2.4 %convolution_bitcast_fusion.1 = f32[4,256,32]{1,2,0:T(8,128)S(1)} fusion(bf16[4,256,1024]{2,1,0:T(8,128)(2,1)} %param.9, bf16[4,32,1024]{2,0,1:T(4,128)(2,1)} %all-to-all-done.1), kind=kOutput, calls=%fused_computation.27 | convolution fusion | flops 67108864 | bytes 2490368 | tf_op jit(solution)/shard_map/imd,isd->ims/dot_general | solution.py:62
  74.0 1.0 fusion.32
  75.0 0.0 copy-start.5
  75.0 6.7 %all-to-all-done.3 = bf16[4,32,1024]{2,0,1:T(4,128)(2,1)S(1)} async-done(((bf16[4,32,1024]{2,0,1:T(4,128)(2,1)}), bf16[4,32,1024]{2,0,1:T(4,128)(2,1)S(1)}, u32[]{:S(2)}, u32[]{:S(2)}) %all-to-all-start.3) | async-done | bytes 262176 | tf_op jit(solution)/shard_map/all_to_all | solution.py:32
  81.7 0.7 convolution_bitcast_fusion
  82.4 0.0 copy-done.4
  82.5 1.2 convolution_bitcast_fusion.2
  83.7 2.8 %fusion.46 = f32[4,256,1024]{2,1,0:T(8,128)} fusion(bf16[4,32,1024]{2,0,1:T(4,128)(2,1)S(1)} %all-to-all-done.3, f32[4,32]{1,0:T(4,128)S(1)} %get-tuple-element.5, f32[4,256,32]{1,2,0:T(8,128)S(1)} %fusion.52), kind=kOutput, calls=%fused_computation.49 | convolution fusion | flops 67207552 | bytes 4588032 | tf_op jit(solution)/shard_map/ims,isd->imd/dot_general | solution.py:81
  86.5 4.5 %add_convert_fusion = bf16[4,256,1024]{2,1,0:T(8,128)(2,1)} fusion(f32[4,256,1024]{2,1,0:T(8,128)} %fusion.46, f32[4,256,32]{1,2,0:T(8,128)S(1)} %fusion.32, f32[4,256,32]{1,2,0:T(8,128)S(1)} %convolution_bitcast_fusion, bf16[1024,32]{0,1:T(8,128)(2,1)S(1)} %copy-done.5, f32[4,256,32]{1,2,0:T(8,128)S(1)} %copy-done.4, f32[4,32]{1,0:T(4,128)S(1)} %get-tuple-element.5), kind=kOutput, calls=%fused_computation.14 | convolution fusion | flops 69435776 | bytes 6750720 | tf_op jit(solution)/shard_map/ims,ds->imd/dot_general | solution.py:82
  91.0 0.0 all-reduce.3.cloned.1.call-update
  91.0 3.0 %convolution_convert_fusion = bf16[4,256,1024]{2,1,0:T(8,128)(2,1)} fusion(bf16[4,32,1024]{2,0,1:T(4,128)(2,1)} %all-to-all-done.1, f32[4,256]{1,0:T(4,128)S(1)} %get-tuple-element.7, f32[4,256,32]{1,2,0:T(8,128)S(1)} %fusion.52), kind=kOutput, calls=%fused_computation.17 | convolution fusion | flops 68256800 | bytes 2494464 | tf_op jit(solution)/shard_map/ims,isd->imd/dot_general | solution.py:55
  94.1 117.5 %all-reduce.3.cloned.1.call-done = f32[1024,32]{0,1:T(8,128)} async-done(((f32[1024,32]{0,1:T(8,128)}), f32[1024,32]{0,1:T(8,128)}) %all-reduce.3.cloned.1.call-update) | async-done | bytes 131088
  211.6 1.4 constant_dynamic-slice_fusion
  (4 shorter events, 0.0 us)
Async XLA Ops:
  7.2 1.6 copy-start
  12.5 17.7 %all-to-all-start = ((bf16[4,32,1024]{2,0,1:T(4,128)(2,1)}), bf16[4,32,1024]{2,0,1:T(4,128)(2,1)S(1)}, u32[]{:S(2)}, u32[]{:S(2)}) async-start(bf16[4,32,1024]{2,0,1:T(4,128)(2,1)} %copy.18), calls=%async_computation | async-start | bytes 524288 | tf_op jit(solution)/shard_map/all_to_all | solution.py:20
  30.2 13.7 %all-to-all-start.2 = ((bf16[4,32,1024]{2,0,1:T(4,128)(2,1)}), bf16[4,32,1024]{2,0,1:T(4,128)(2,1)}, u32[]{:S(2)}, u32[]{:S(2)}) async-start(bf16[4,32,1024]{2,0,1:T(4,128)(2,1)} %copy.22), calls=%async_computation.2 | async-start | bytes 524288 | tf_op jit(solution)/shard_map/all_to_all | solution.py:28
  33.5 3.5 %copy-start.7 = (bf16[1,2048,1024]{2,1,0:T(8,128)(2,1)S(1)}, bf16[1,2048,1024]{2,1,0:T(8,128)(2,1)}, u32[]{:S(2)}) copy-start(bf16[1,2048,1024]{2,1,0:T(8,128)(2,1)} %param.8) | copy-start | bytes 12582916
  44.9 4.9 %copy-start.2 = (bf16[4,32,1024]{2,1,0:T(8,128)(2,1)}, bf16[4,32,1024]{2,1,0:T(8,128)(2,1)S(1)}, u32[]{:S(2)}) copy-start(bf16[4,32,1024]{2,1,0:T(8,128)(2,1)S(1)} %copy.23) | copy-start | bytes 786436
  44.9 4.9 %copy-start.6 = (bf16[128,1024]{1,0:T(8,128)(2,1)S(1)}, bf16[128,1024]{1,0:T(8,128)(2,1)}, u32[]{:S(2)}) copy-start(bf16[128,1024]{1,0:T(8,128)(2,1)} %fusion.21) | copy-start | bytes 786436
  50.8 14.8 %all-to-all-start.1 = ((bf16[4,32,1024]{2,0,1:T(4,128)(2,1)}), bf16[4,32,1024]{2,0,1:T(4,128)(2,1)}, u32[]{:S(2)}, u32[]{:S(2)}) async-start(bf16[4,32,1024]{2,0,1:T(4,128)(2,1)} %copy.20), calls=%async_computation.1 | async-start | bytes 524288 | tf_op jit(solution)/shard_map/all_to_all | solution.py:24
  54.1 4.9 %copy-start.1 = (bf16[128,2048]{1,0:T(8,128)(2,1)S(1)}, bf16[128,2048]{1,0:T(8,128)(2,1)}, u32[]{:S(2)}) copy-start(bf16[128,2048]{1,0:T(8,128)(2,1)} %fusion.15) | copy-start | bytes 1572868
  54.1 8.1 %copy-start.3 = (bf16[4,32,1024]{2,1,0:T(8,128)(2,1)S(1)}, bf16[4,32,1024]{2,1,0:T(8,128)(2,1)}, u32[]{:S(2)}) copy-start(bf16[4,32,1024]{2,1,0:T(8,128)(2,1)} %copy-done.2) | copy-start | bytes 786436
  65.6 16.9 %copy-start.4 = (f32[4,256,32]{1,2,0:T(8,128)S(1)}, f32[4,256,32]{1,2,0:T(8,128)}, u32[]{:S(2)}) copy-start(f32[4,256,32]{1,2,0:T(8,128)} %get-tuple-element.6) | copy-start | bytes 393220
  65.6 16.2 %all-to-all-start.3 = ((bf16[4,32,1024]{2,0,1:T(4,128)(2,1)}), bf16[4,32,1024]{2,0,1:T(4,128)(2,1)S(1)}, u32[]{:S(2)}, u32[]{:S(2)}) async-start(bf16[4,32,1024]{2,0,1:T(4,128)(2,1)} %copy.24), calls=%async_computation.3 | async-start | bytes 524288 | tf_op jit(solution)/shard_map/all_to_all | solution.py:32
  71.3 140.2 %all-reduce.3.cloned.1.call-start = ((), (), s32[]{:S(2)}) async-start(), calls=%async_computation.4 | async-start | bytes 262144
  75.0 11.5 %copy-start.5 = (bf16[1024,32]{0,1:T(8,128)(2,1)S(1)}, bf16[1024,32]{0,1:T(8,128)(2,1)}, u32[]{:S(2)}) copy-start(bf16[1024,32]{0,1:T(8,128)(2,1)} %param.6) | copy-start | bytes 196612
Sparse Core Ops, SparseCore 0:
  91.2 120.3 all-reduce.2
where the time goes:
time: 220 us
  waiting for transfers between devices  136 us (62%)
  matrix products  38.9 us (18%)
  starting transfers between devices  19.9 us (9%)
  between operations  14.2 us (6%)
  local copies, waits for them, and re-layouts  8.05 us (4%)
  other arithmetic  2.51 us (1%)
    unnamed x2, waiting for transfers between devices  118 us
    all_to_all x1, starting transfers between devices, send_slots(): lax.all_to_all(slots, ('row', 'col'), split_axis=1, concat_axis=1, tiled=...  7.3 us
    all_to_all x1, waiting for transfers between devices, send_slots(): lax.all_to_all(slots, ('row', 'col'), split_axis=1, concat_axis=1, tiled=...  6.71 us
    all_to_all x1, waiting for transfers between devices, return_in_grads(): lax.all_to_all(slots, ('row', 'col'), split_axis=1, concat_axis=1, tiled=...  6.69 us
    all_to_all x1, starting transfers between devices, return_in_grads(): lax.all_to_all(slots, ('row', 'col'), split_axis=1, concat_axis=1, tiled=...  5.76 us
    all_to_all x1, waiting for transfers between devices, send_out_grads(): lax.all_to_all(slots, ('row', 'col'), split_axis=1, concat_axis=1, tiled=...  5.3 us
    dot_general x1, matrix products, on_device(): jnp.einsum('rd,hd->rh', grad_rows, weight_b, preferred_element_type=f32)  4.91 us
    dot_general x1, matrix products, on_device(): jnp.einsum('ims,ds->imd', d_logits, phi, preferred_element_type=f32)  4.47 us
  transfers between devices with their start and end apart: 5, of which 4 were waited for; matrix products, arithmetic and copies ran while one was open for 12% of the time, Pallas kernels for 0%

commit v1 on v0

--- a/solution.py
+++ b/solution.py
@@ -17,7 +17,16 @@
 
 
 def send_slots(slots):
-    return lax.all_to_all(slots, ("row", "col"), split_axis=1, concat_axis=1, tiled=True)
+
+    def trace_field_on_mesh(lane_axis, work_x):
+        return jnp.concatenate(
+            lax.all_to_all(
+                jnp.stack(jnp.split(work_x, lax.axis_size(lane_axis), 1)), lane_axis, 0, 0
+            ),
+            axis=1,
+        )
+
+    return trace_field_on_mesh(("row", "col"), slots)
 
 
 def return_results(slots):

time: 220 us -> 232 us (1.055)
  local copies, waits for them, and re-layouts: 8.05 us -> 27 us
  waiting for transfers between devices: 136 us -> 129 us
    unnamed x17 -> x48, local copies, waits for them, and re-layouts: 3.28 us -> 22 us
    unnamed x2, waiting for transfers between devices: 118 us -> 110 us
  transfers between devices with their start and end apart: 5 -> 5, of which waited for: 4 -> 4; matrix products, arithmetic and copies ran while one was open for 12% -> 15% of each run, Pallas kernels for 0% -> 0%
where the time goes in v1:
time: 232 us; the launch traced here: 231 us
  waiting for transfers between devices  129 us (56%)
  matrix products  39 us (17%)
  local copies, waits for them, and re-layouts  27 us (12%)
  starting transfers between devices  19.9 us (9%)
  between operations  14.2 us (6%)
  other arithmetic  2.51 us (1%)
    unnamed x2, waiting for transfers between devices  110 us
    unnamed x48, local copies, waits for them, and re-layouts  22 us
    all_to_all x1, starting transfers between devices, trace_field_on_mesh(): lax.all_to_all(jnp.stack(jnp.split(work_x, lax.axis_size(lane_axis), 1)),...  7.3 us
    all_to_all x1, waiting for transfers between devices, trace_field_on_mesh(): lax.all_to_all(jnp.stack(jnp.split(work_x, lax.axis_size(lane_axis), 1)),...  6.71 us
    all_to_all x1, waiting for transfers between devices, return_in_grads(): lax.all_to_all(slots, ('row', 'col'), split_axis=1, concat_axis=1, tiled=...  6.69 us
    all_to_all x1, starting transfers between devices, return_in_grads(): lax.all_to_all(slots, ('row', 'col'), split_axis=1, concat_axis=1, tiled=...  5.76 us
    all_to_all x1, waiting for transfers between devices, send_out_grads(): lax.all_to_all(slots, ('row', 'col'), split_axis=1, concat_axis=1, tiled=...  5.3 us
    dot_general x1, matrix products, on_device(): jnp.einsum('rd,hd->rh', grad_rows, weight_b, preferred_element_type=f32)  4.91 us
  transfers between devices with their start and end apart: 5, of which 4 were waited for; matrix products, arithmetic and copies ran while one was open for 15% of the time, Pallas kernels for 0%

profile of v1, /device:TPU:0, one launch (start us, length us, event | category | flops | bytes accessed | tf_op | source)
XLA Modules:
  0.0 231.4 jit_solution(11266313475788168160)
XLA Ops:
  7.2 1.6 copy-done
  8.8 1.6 fusion.52
  10.3 0.8 fusion.62
  12.2 0.6 constant_dynamic-update-slice_fusion.31
  14.0 0.6 constant_dynamic-update-slice_fusion.28
  14.6 0.6 constant_dynamic-update-slice_fusion.27
  15.2 0.6 constant_dynamic-update-slice_fusion.26
  15.8 0.6 constant_dynamic-update-slice_fusion.25
  16.4 0.6 constant_dynamic-update-slice_fusion.24
  17.0 0.6 constant_dynamic-update-slice_fusion.23
  20.0 0.6 constant_dynamic-update-slice_fusion.18
  20.6 0.6 constant_dynamic-update-slice_fusion.17
  21.2 0.6 constant_dynamic-update-slice_fusion.16
  21.8 0.6 constant_dynamic-update-slice_fusion.15
  22.4 0.6 constant_dynamic-update-slice_fusion.14
  25.4 0.6 constant_dynamic-update-slice_fusion.9
  26.0 0.6 constant_dynamic-update-slice_fusion.8
  26.6 0.6 constant_dynamic-update-slice_fusion.7
  27.2 0.6 constant_dynamic-update-slice_fusion.6
  27.8 0.6 constant_dynamic-update-slice_fusion.5
  31.5 7.3 %all-to-all-start = ((bf16[32,4,1,1024]{3,1,2,0:T(4,128)(2,1)}), bf16[32,4,1,1024]{3,1,2,0:T(4,128)(2,1)S(1)}, u32[]{:S(2)}, u32[]{:S(2)}) async-start(bf16[32,4,1,1024]{3,1,2,0:T(4,128)(2,1)} %constant_dynamic-update-slice_fusion), calls=%async_computation | async-start | bytes 524288 | tf_op jit(solution)/shard_map/all_to_all | solution.py:23
  38.8 0.7 fusion.63
  39.5 2.0 convolution_convert_fusion.1
  41.5 0.9 copy.540
  42.4 6.7 %all-to-all-done = bf16[32,4,1,1024]{3,1,2,0:T(4,128)(2,1)S(1)} async-done(((bf16[32,4,1,1024]{3,1,2,0:T(4,128)(2,1)}), bf16[32,4,1,1024]{3,1,2,0:T(4,128)(2,1)S(1)}, u32[]{:S(2)}, u32[]{:S(2)}) %all-to-all-start) | async-done | bytes 262176 | tf_op jit(solution)/shard_map/all_to_all | solution.py:23
  49.2 3.3 %all-to-all-start.2 = ((bf16[4,32,1024]{2,0,1:T(4,128)(2,1)}), bf16[4,32,1024]{2,0,1:T(4,128)(2,1)}, u32[]{:S(2)}, u32[]{:S(2)}) async-start(bf16[4,32,1024]{2,0,1:T(4,128)(2,1)} %copy.540), calls=%async_computation.2 | async-start | bytes 524288 | tf_op jit(solution)/shard_map/all_to_all | solution.py:37
  52.6 3.1 %fusion.10 = f32[128,2048]{1,0:T(8,128)S(1)} fusion(bf16[128,1024]{1,0:T(8,128)(2,1)S(1)} %bitcast.122, bf16[1,1024,2048]{2,1,0:T(8,128)(2,1)} %param.7), kind=kOutput, calls=%fused_computation.10 | convolution fusion | flops 536870912 | bytes 5505024 | tf_op jit(solution)/shard_map/dot_general | solution.py:59
  55.9 1.6 fusion.21
  57.5 5.3 %all-to-all-done.2 = bf16[4,32,1024]{2,0,1:T(4,128)(2,1)} async-done(((bf16[4,32,1024]{2,0,1:T(4,128)(2,1)}), bf16[4,32,1024]{2,0,1:T(4,128)(2,1)}, u32[]{:S(2)}, u32[]{:S(2)}) %all-to-all-start.2) | async-done | bytes 262176 | tf_op jit(solution)/shard_map/all_to_all | solution.py:37
  62.8 1.0 copy.541
  63.9 4.9 %fusion.15 = bf16[128,2048]{1,0:T(8,128)(2,1)} fusion(bf16[128,1024]{1,0:T(8,128)(2,1)S(1)} %bitcast.124, bf16[1,2048,1024]{2,1,0:T(8,128)(2,1)} %param.8, f32[128,2048]{1,0:T(8,128)S(1)} %fusion.10), kind=kOutput, calls=%fused_computation.16 | convolution fusion | flops 541851648 | bytes 6029312 | tf_op jit(solution)/shard_map/rd,hd->rh/dot_general | solution.py:76
  68.8 0.9 copy.538
  69.7 3.3 %all-to-all-start.1 = ((bf16[4,32,1024]{2,0,1:T(4,128)(2,1)}), bf16[4,32,1024]{2,0,1:T(4,128)(2,1)}, u32[]{:S(2)}, u32[]{:S(2)}) async-start(bf16[4,32,1024]{2,0,1:T(4,128)(2,1)} %copy.538), calls=%async_computation.1 | async-start | bytes 524288 | tf_op jit(solution)/shard_map/all_to_all | solution.py:33
  73.1 3.9 %fusion.18 = bf16[128,1024]{1,0:T(8,128)(2,1)S(1)} fusion(bf16[128,2048]{1,0:T(8,128)(2,1)} %fusion.15, bf16[1,1024,2048]{2,1,0:T(8,128)(2,1)} %param.7), kind=kOutput, calls=%fused_computation.22 | convolution fusion | flops 537001984 | bytes 4980736 | tf_op jit(solution)/shard_map/rh,dh->rd/dot_general | solution.py:81
  77.0 0.9 copy.542
  77.9 3.3 %convert_bitcast_fusion.1 = bf16[1,1024,2048]{2,1,0:T(8,128)(2,1)} fusion(bf16[128,1024]{1,0:T(8,128)(2,1)S(1)} %bitcast.123, bf16[128,2048]{1,0:T(8,128)(2,1)S(1)} %copy-done.1), kind=kOutput, calls=%fused_computation.13 | convolution fusion | flops 538968064 | bytes 4980736 | tf_op jit(solution)/shard_map/rd,rh->dh/dot_general | solution.py:78
  81.2 3.3 %convert_bitcast_fusion = bf16[1,2048,1024]{2,1,0:T(8,128)(2,1)} fusion(bf16[128,1024]{1,0:T(8,128)(2,1)S(1)} %bitcast.125, f32[128,2048]{1,0:T(8,128)S(1)} %fusion.10), kind=kOutput, calls=%fused_computation.12 | convolution fusion | flops 541327360 | bytes 5505024 | tf_op jit(solution)/shard_map/rh,rd->hd/dot_general | solution.py:73
  84.5 5.8 %all-to-all-start.3 = ((bf16[4,32,1024]{2,0,1:T(4,128)(2,1)}), bf16[4,32,1024]{2,0,1:T(4,128)(2,1)S(1)}, u32[]{:S(2)}, u32[]{:S(2)}) async-start(bf16[4,32,1024]{2,0,1:T(4,128)(2,1)} %copy.542), calls=%async_computation.3 | async-start | bytes 524288 | tf_op jit(solution)/shard_map/all_to_all | solution.py:41
  90.5 2.4 %convolution_bitcast_fusion.1 = f32[4,256,32]{1,2,0:T(8,128)S(1)} fusion(bf16[4,256,1024]{2,1,0:T(8,128)(2,1)} %param.9, bf16[4,32,1024]{2,0,1:T(4,128)(2,1)} %all-to-all-done.1), kind=kOutput, calls=%fused_computation.27 | convolution fusion | flops 67108864 | bytes 2490368 | tf_op jit(solution)/shard_map/imd,isd->ims/dot_general | solution.py:71
  92.9 1.0 fusion.32
  94.0 6.7 %all-to-all-done.3 = bf16[4,32,1024]{2,0,1:T(4,128)(2,1)S(1)} async-done(((bf16[4,32,1024]{2,0,1:T(4,128)(2,1)}), bf16[4,32,1024]{2,0,1:T(4,128)(2,1)S(1)}, u32[]{:S(2)}, u32[]{:S(2)}) %all-to-all-start.3) | async-done | bytes 262176 | tf_op jit(solution)/shard_map/all_to_all | solution.py:41
  100.7 0.7 convolution_bitcast_fusion
  101.4 1.2 convolution_bitcast_fusion.2
  102.7 2.8 %fusion.46 = f32[4,256,1024]{2,1,0:T(8,128)} fusion(bf16[4,32,1024]{2,0,1:T(4,128)(2,1)S(1)} %all-to-all-done.3, f32[4,32]{1,0:T(4,128)S(1)} %get-tuple-element.37, f32[4,256,32]{1,2,0:T(8,128)S(1)} %fusion.52), kind=kOutput, calls=%fused_computation.49 | convolution fusion | flops 67207552 | bytes 4588032 | tf_op jit(solution)/shard_map/ims,isd->imd/dot_general | solution.py:90
  105.5 4.5 %add_convert_fusion = bf16[4,256,1024]{2,1,0:T(8,128)(2,1)} fusion(f32[4,256,1024]{2,1,0:T(8,128)} %fusion.46, f32[4,256,32]{1,2,0:T(8,128)S(1)} %fusion.32, f32[4,256,32]{1,2,0:T(8,128)S(1)} %convolution_bitcast_fusion, bf16[1024,32]{0,1:T(8,128)(2,1)S(1)} %copy-done.5, f32[4,256,32]{1,2,0:T(8,128)S(1)} %copy-done.4, f32[4,32]{1,0:T(4,128)S(1)} %get-tuple-element.37), kind=kOutput, calls=%fused_computation.14 | convolution fusion | flops 69435776 | bytes 6750720 | tf_op jit(solution)/shard_map/ims,ds->imd/dot_general | solution.py:91
  110.0 3.0 %convolution_convert_fusion = bf16[4,256,1024]{2,1,0:T(8,128)(2,1)} fusion(bf16[4,32,1024]{2,0,1:T(4,128)(2,1)} %all-to-all-done.1, f32[4,256]{1,0:T(4,128)S(1)} %get-tuple-element.39, f32[4,256,32]{1,2,0:T(8,128)S(1)} %fusion.52), kind=kOutput, calls=%fused_computation.17 | convolution fusion | flops 68256800 | bytes 2494464 | tf_op jit(solution)/shard_map/ims,isd->imd/dot_general | solution.py:64
  113.0 110.1 %all-reduce.3.cloned.1.call-done = f32[1024,32]{0,1:T(8,128)} async-done(((f32[1024,32]{0,1:T(8,128)}), f32[1024,32]{0,1:T(8,128)}) %all-reduce.3.cloned.1.call-update) | async-done | bytes 131088
  223.2 1.4 constant_dynamic-slice_fusion
  (37 shorter events, 10.8 us)
Async XLA Ops:
  7.2 1.6 copy-start
  31.5 17.7 %all-to-all-start = ((bf16[32,4,1,1024]{3,1,2,0:T(4,128)(2,1)}), bf16[32,4,1,1024]{3,1,2,0:T(4,128)(2,1)S(1)}, u32[]{:S(2)}, u32[]{:S(2)}) async-start(bf16[32,4,1,1024]{3,1,2,0:T(4,128)(2,1)} %constant_dynamic-update-slice_fusion), calls=%async_computation | async-start | bytes 524288 | tf_op jit(solution)/shard_map/all_to_all | solution.py:23
  49.2 13.7 %all-to-all-start.2 = ((bf16[4,32,1024]{2,0,1:T(4,128)(2,1)}), bf16[4,32,1024]{2,0,1:T(4,128)(2,1)}, u32[]{:S(2)}, u32[]{:S(2)}) async-start(bf16[4,32,1024]{2,0,1:T(4,128)(2,1)} %copy.540), calls=%async_computation.2 | async-start | bytes 524288 | tf_op jit(solution)/shard_map/all_to_all | solution.py:37
  52.5 3.5 %copy-start.7 = (bf16[1,2048,1024]{2,1,0:T(8,128)(2,1)S(1)}, bf16[1,2048,1024]{2,1,0:T(8,128)(2,1)}, u32[]{:S(2)}) copy-start(bf16[1,2048,1024]{2,1,0:T(8,128)(2,1)} %param.8) | copy-start | bytes 12582916
  63.9 4.9 %copy-start.2 = (bf16[4,32,1024]{2,1,0:T(8,128)(2,1)}, bf16[4,32,1024]{2,1,0:T(8,128)(2,1)S(1)}, u32[]{:S(2)}) copy-start(bf16[4,32,1024]{2,1,0:T(8,128)(2,1)S(1)} %copy.541) | copy-start | bytes 786436
  63.9 4.9 %copy-start.6 = (bf16[128,1024]{1,0:T(8,128)(2,1)S(1)}, bf16[128,1024]{1,0:T(8,128)(2,1)}, u32[]{:S(2)}) copy-start(bf16[128,1024]{1,0:T(8,128)(2,1)} %fusion.21) | copy-start | bytes 786436
  69.7 14.8 %all-to-all-start.1 = ((bf16[4,32,1024]{2,0,1:T(4,128)(2,1)}), bf16[4,32,1024]{2,0,1:T(4,128)(2,1)}, u32[]{:S(2)}, u32[]{:S(2)}) async-start(bf16[4,32,1024]{2,0,1:T(4,128)(2,1)} %copy.538), calls=%async_computation.1 | async-start | bytes 524288 | tf_op jit(solution)/shard_map/all_to_all | solution.py:33
  73.0 4.9 %copy-start.1 = (bf16[128,2048]{1,0:T(8,128)(2,1)S(1)}, bf16[128,2048]{1,0:T(8,128)(2,1)}, u32[]{:S(2)}) copy-start(bf16[128,2048]{1,0:T(8,128)(2,1)} %fusion.15) | copy-start | bytes 1572868
  73.0 8.1 %copy-start.3 = (bf16[4,32,1024]{2,1,0:T(8,128)(2,1)S(1)}, bf16[4,32,1024]{2,1,0:T(8,128)(2,1)}, u32[]{:S(2)}) copy-start(bf16[4,32,1024]{2,1,0:T(8,128)(2,1)} %copy-done.2) | copy-start | bytes 786436
  84.5 16.9 %copy-start.4 = (f32[4,256,32]{1,2,0:T(8,128)S(1)}, f32[4,256,32]{1,2,0:T(8,128)}, u32[]{:S(2)}) copy-start(f32[4,256,32]{1,2,0:T(8,128)} %get-tuple-element.38) | copy-start | bytes 393220
  84.5 16.2 %all-to-all-start.3 = ((bf16[4,32,1024]{2,0,1:T(4,128)(2,1)}), bf16[4,32,1024]{2,0,1:T(4,128)(2,1)S(1)}, u32[]{:S(2)}, u32[]{:S(2)}) async-start(bf16[4,32,1024]{2,0,1:T(4,128)(2,1)} %copy.542), calls=%async_computation.3 | async-start | bytes 524288 | tf_op jit(solution)/shard_map/all_to_all | solution.py:41
  90.3 132.9 %all-reduce.3.cloned.1.call-start = ((), (), s32[]{:S(2)}) async-start(), calls=%async_computation.4 | async-start | bytes 262144
  94.0 11.6 %copy-start.5 = (bf16[1024,32]{0,1:T(8,128)(2,1)S(1)}, bf16[1024,32]{0,1:T(8,128)(2,1)}, u32[]{:S(2)}) copy-start(bf16[1024,32]{0,1:T(8,128)(2,1)} %param.6) | copy-start | bytes 196612
Sparse Core Ops, SparseCore 0:
  102.8 120.3 all-reduce.2
